TPU v7x, 32 devices: a whole 2x2x4 slice. The times are simulated.
32 devices in a mesh: sub: 2 (over y), rng: 16 (over z, x, core).
Axes of the slice: x: 2, y: 2, z: 4, core: 2. Of those that a mesh axis runs over, the one named last changes fastest.
Arguments:
- echoes: bfloat16 [2, 1024, 8192], P(None, ('sub', 'rng')), may hold values from -6 to 6
- fore_flag: int32 [1, 2, 16], P(None, None, 'rng'), may hold values from 0 to 1, as said below
- band_offset: int32 [1, 2, 16], P(None, None, 'rng'), may hold values from -16 to 16, as said below
- angle_interp: bfloat16 [1, 2, 512, 256], replicated, may hold values from -1 to 1
- range_kernel: bfloat16 [1, 544, 512], replicated, may hold values from -1 to 2, as said below
- center_shift: float32 [1, 2], replicated, may hold values from -6 to 6
Outputs:
- focused_image: float32 [2, 1024, 8192], P(None, 'sub', 'rng')
Inputs may be any that keep to these rules, and one draw needn't show every extreme that they name: fore_flag[l, g, b] + fore_flag[l, g XOR 2**l, b] = 1 for every level l, group g and block b. `band_offset`: in every level both -16 and 16 occur. range_kernel[l, w, r] = 0 wherever |w - 16 - r| > 16.
All inputs are finite; a program needn't handle non-finite values.
Results may differ from a plain program's by a relative error of at most 0.0076.
Values may be sent and summed in bfloat16 or wider, within the bound.
No kernel may reach another device: no remote copies, remote signals or barrier semaphores. Data moves between devices by JAX's collectives and lax.ppermute only.
A program may use at most 64 MiB of HBM per device.

v0:
```python
import math

import jax
import jax.numpy as jnp
from jax import lax
from jax.sharding import PartitionSpec as P

ANGLES = 512
PULSES = 512
BAND_HALF = 16
RIM_WIDTH = 32


def padded(value, sides, width):
    for axis, dim in sides:
        devices, length = (lax.axis_size(axis), value.shape[dim])
        up = [(i, (i + 1) % devices) for i in range(devices - 1)]
        down = [(j, i) for i, j in up]
        last = lax.slice_in_dim(value, length - width, length, axis=dim)
        leading = lax.slice_in_dim(value, 0, width, axis=dim)
        before = lax.ppermute(last, axis, up)
        after = lax.ppermute(leading, axis, down)
        value = jnp.concatenate([before, value, after], axis=dim)
    return value


def from_partner(value, axis, apart):
    mask = 2**apart
    pairs = [(source, source ^ mask) for source in range(lax.axis_size(axis))]
    return lax.ppermute(value, axis, pairs)


def doppler_matrix(angles, pulses):
    angle_ids = jnp.arange(angles, dtype=jnp.int32)[:, None]
    pulse_ids = jnp.arange(pulses, dtype=jnp.int32)[None, :]
    cycles = (2 * angle_ids + 1 - angles) * pulse_ids % (2 * angles)
    phase_angle = math.pi / angles * cycles.astype(jnp.float32)
    cosine = jnp.cos(phase_angle) / math.sqrt(pulses)
    sine_part = jnp.sin(phase_angle) / math.sqrt(pulses)
    upper_rows = jnp.concatenate([cosine, sine_part], axis=1)
    bottom = jnp.concatenate([-sine_part, cosine], axis=1)
    return jnp.concatenate([upper_rows, bottom], axis=0).astype(jnp.bfloat16)


def phase_turn(real_imag, shift_rate, block_start, total_bins):
    angles = real_imag.shape[1]
    bin_count = real_imag.shape[2]
    angle_pos = (jnp.arange(angles).astype(jnp.float32)[:, None] + 0.5) / angles - 0.5
    range_pos = (
        1.0 + (block_start + jnp.arange(bin_count)).astype(jnp.float32)[None, :] / total_bins
    )
    phase_angle = math.pi * shift_rate * angle_pos * range_pos
    cosine = jnp.cos(phase_angle)
    sine_part = jnp.sin(phase_angle)
    real_part = real_imag[0] * cosine - real_imag[1] * sine_part
    imag_part = real_imag[0] * sine_part + real_imag[1] * cosine
    return jnp.stack([real_part, imag_part])


def on_device(echoes, fore_flag, band_offset, angle_interp, range_kernel, center_shift):
    group_index = lax.axis_index("sub")
    block_index = lax.axis_index("rng")
    sub_count = lax.axis_size("sub")
    rng_count = lax.axis_size("rng")
    local_pulses = echoes.shape[1]
    block_bins = echoes.shape[2] // rng_count
    total_bins = block_bins * rng_count
    block_start = block_index * block_bins
    filter_matrix = doppler_matrix(ANGLES, PULSES)
    split_echoes = echoes.reshape(2, local_pulses, rng_count, block_bins)
    received = lax.all_to_all(split_echoes, "rng", split_axis=2, concat_axis=1, tiled=True)
    columns = received.shape[3]
    stacked = received.reshape(2 * PULSES, columns)
    filtered = jnp.dot(filter_matrix, stacked, preferred_element_type=jnp.float32)
    sector_image = filtered.astype(jnp.bfloat16).reshape(2, ANGLES, columns)
    levels = min(3, sub_count // 2)
    half_rows = ANGLES // 2
    group_ids = jnp.arange(sub_count, dtype=jnp.int32)
    for tree_level in range(levels):
        stride = 2**tree_level
        upper_side = group_index // stride % 2
        partner = group_index + (1 - 2 * upper_side) * stride
        own_mask = group_ids == group_index
        partner_mask = group_ids == partner
        own_flag = jnp.sum(jnp.where(own_mask, fore_flag[tree_level, :, 0], 0))
        partner_flag = 1 - own_flag
        own_shift = jnp.sum(jnp.where(own_mask, center_shift[tree_level], 0.0))
        partner_shift = jnp.sum(jnp.where(partner_mask, center_shift[tree_level], 0.0))
        offset = jnp.sum(jnp.where(own_mask, band_offset[tree_level, :, 0], 0))
        extended = padded(sector_image, (("rng", 2),), RIM_WIDTH)
        window = lax.dynamic_slice_in_dim(
            extended, RIM_WIDTH - BAND_HALF + offset, block_bins + 2 * BAND_HALF, 2
        )
        resampled = jnp.einsum(
            "caw,wr->car", window, range_kernel[tree_level], preferred_element_type=jnp.float32
        ).astype(jnp.bfloat16)
        own_rows = lax.dynamic_slice_in_dim(resampled, own_flag * half_rows, half_rows, 1)
        outgoing = lax.dynamic_slice_in_dim(resampled, partner_flag * half_rows, half_rows, 1)
        partner_rows = from_partner(outgoing, "sub", tree_level)
        own_matrix = lax.dynamic_index_in_dim(angle_interp[tree_level], own_flag, 0, keepdims=False)
        partner_matrix = lax.dynamic_index_in_dim(
            angle_interp[tree_level], partner_flag, 0, keepdims=False
        )
        own_term = jnp.einsum(
            "pa,car->cpr", own_matrix, own_rows, preferred_element_type=jnp.float32
        )
        partner_term = jnp.einsum(
            "pa,car->cpr", partner_matrix, partner_rows, preferred_element_type=jnp.float32
        )
        merged = phase_turn(own_term, own_shift, block_start, total_bins)
        merged = merged + phase_turn(partner_term, partner_shift, block_start, total_bins)
        if tree_level + 1 < levels:
            sector_image = merged.astype(jnp.bfloat16)
        else:
            sector_image = merged
    return sector_image


def solution(mesh):
    placed = (
        P(None, ("sub", "rng"), None),
        P(None, None, "rng"),
        P(None, None, "rng"),
        P(),
        P(),
        P(),
    )
    return jax.shard_map(
        on_device, mesh=mesh, in_specs=placed, out_specs=P(None, "sub", "rng"), check_vma=False
    )
```

profile of v0, /device:TPU:10, one launch (start us, length us, event | category | flops | bytes accessed | tf_op | source)
XLA Modules:
  0.0 70.7 jit_solution(14458601255348271940)
XLA Ops:
  0.0 0.0 copy-start
  0.0 0.0 copy-start.5
  0.0 2.4 %copy.38 = bf16[2,4,16,8,512]{4,3,1,0,2:T(8,128)(2,1)} copy(bf16[2,4,16,8,512]{4,3,2,1,0:T(8,128)(2,1)} %bitcast.43) | data formatting | bytes 2097152 | tf_op jit(solution)/shard_map/reshape | solution.py:70
  2.4 6.2 %all-to-all-start = ((bf16[2,32,16,512]{3,1,0,2:T(8,128)(2,1)}), bf16[2,32,16,512]{3,1,0,2:T(8,128)(2,1)S(1)}, u32[]{:S(2)}, u32[]{:S(2)}) async-start(bf16[2,32,16,512]{3,1,0,2:T(8,128)(2,1)} %bitcast.42), calls=%async_computation | async-start | bytes 2097152 | tf_op jit(solution)/shard_map/all_to_all | solution.py:71
  8.7 0.0 copy-done.5
  8.7 0.6 fusion.47
  10.4 5.7 %fusion.32 = (bf16[512,512]{1,0:T(8,128)(2,1)S(1)}, bf16[512,512]{1,0:T(8,128)(2,1)}, bf16[512,512]{1,0:T(8,128)(2,1)}) fusion(s32[512]{0:T(512)S(1)} %multiply_add_fusion.2), kind=kLoop, calls=%fused_computation.47 | loop fusion | flops 5242880 | bytes 1574912 | tf_op jit(solution)/shard_map/convert.5
  16.2 17.2 %all-to-all-done = bf16[2,32,16,512]{3,1,0,2:T(8,128)(2,1)S(1)} async-done(((bf16[2,32,16,512]{3,1,0,2:T(8,128)(2,1)}), bf16[2,32,16,512]{3,1,0,2:T(8,128)(2,1)S(1)}, u32[]{:S(2)}, u32[]{:S(2)}) %all-to-all-start) | async-done | bytes 1048608 | tf_op jit(solution)/shard_map/all_to_all | solution.py:71
  33.4 0.0 copy-start.1
  33.4 0.0 copy-start.2
  33.4 0.1 copy.27
  33.5 0.9 %copy-done.1 = bf16[512,512]{1,0:T(8,128)(2,1)S(1)} copy-done((bf16[512,512]{1,0:T(8,128)(2,1)S(1)}, bf16[512,512]{1,0:T(8,128)(2,1)}, u32[]{:S(2)}) %copy-start.1) | copy-done | bytes 524312
  34.4 0.2 copy-done.2
  34.6 1.2 %fusion.8 = bf16[1024,512]{1,0:T(8,128)(2,1)S(1)} fusion(bf16[1024,512]{1,0:T(8,128)(2,1)S(1)} %bitcast.44, bf16[512,512]{1,0:T(8,128)(2,1)S(1)} %copy-done.2, bf16[512,512]{1,0:T(8,128)(2,1)S(1)} %copy-done.1, bf16[512,512]{1,0:T(8,128)(2,1)S(1)} %get-tuple-element.15), kind=kOutput, calls=%fused_computation.18 | convolution fusion | flops 1082654720 | bytes 3670016 | tf_op jit(solution)/shard_map/dot_general | solution.py:74
  35.8 0.0 copy-start.6
  35.8 0.5 copy.28
  36.4 2.3 %collective-permute-start.1 = (bf16[2,512,32]{1,2,0:T(8,128)(2,1)S(1)}, bf16[2,512,32]{1,2,0:T(8,128)(2,1)S(1)}, u32[]{:S(2)}, u32[]{:S(2)}) collective-permute-start(bf16[2,512,32]{1,2,0:T(8,128)(2,1)S(1)} %get-tuple-element.11), channel_id=1, source_target_pairs={{1,0},{2,1},{3,2},{4,3},{5,4},{6,5},{7,6},{8,7},{9,8},{10,9},{11,1... | collective-permute-start | bytes 196616 | tf_op jit(solution)/shard_map/ppermute | solution.py:22
  38.8 2.0 %collective-permute-start = (bf16[2,512,32]{1,2,0:T(8,128)(2,1)S(1)}, bf16[2,512,32]{1,2,0:T(8,128)(2,1)S(1)}, u32[]{:S(2)}, u32[]{:S(2)}) collective-permute-start(bf16[2,512,32]{1,2,0:T(8,128)(2,1)S(1)} %get-tuple-element.12), channel_id=1, source_target_pairs={{0,1},{1,2},{2,3},{3,4},{4,5},{5,6},{6,7},{7,8},{8,9},{9,10},{10,1... | collective-permute-start | bytes 196616 | tf_op jit(solution)/shard_map/ppermute | solution.py:21
  40.8 0.0 copy-done.6
  40.8 0.6 fusion.46
  42.1 0.0 copy-start.4
  42.1 0.0 copy-start.3
  42.1 0.0 collective-permute-done.1
  42.1 2.2 %collective-permute-done = bf16[2,512,32]{1,2,0:T(8,128)(2,1)S(1)} collective-permute-done((bf16[2,512,32]{1,2,0:T(8,128)(2,1)S(1)}, bf16[2,512,32]{1,2,0:T(8,128)(2,1)S(1)}, u32[]{:S(2)}, u32[]{:S(2)}) %collective-permute-start) | collective-permute-done | bytes 65568 | tf_op jit(solution)/shard_map/ppermute | solution.py:21
  44.3 0.0 copy-done
  44.3 1.3 %convolution_convert_fusion = bf16[2,512,512]{2,1,0:T(8,128)(2,1)S(1)} fusion(s32[]{:T(128)S(6)} %select_n.53, bf16[2,512,32]{1,2,0:T(8,128)(2,1)S(1)} %collective-permute-done, bf16[2,512,512]{1,2,0:T(8,128)(2,1)S(1)} %copy.28, bf16[2,512,32]{1,2,0:T(8,128)(2,1)S(1)} %collective-permute-done.1, bf16[1,544,512]{2,1,0:T(8,128)(2,1)S(1)} %copy-done), kind=kOutput, calls=%fused_computation.19 | convolution fusion | flops 574291968 | bytes 2785284 | tf_op jit(solution)/shard_map/caw,wr->car/dot_general | solution.py:94
  45.7 1.6 %collective-permute-start.2 = (bf16[2,256,512]{2,1,0:T(8,128)(2,1)S(1)}, bf16[2,256,512]{2,1,0:T(8,128)(2,1)S(1)}, u32[]{:S(2)}, u32[]{:S(2)}) collective-permute-start(bf16[2,256,512]{2,1,0:T(8,128)(2,1)S(1)} %constant_dynamic-slice_fusion), channel_id=1, source_target_pairs={{0,16},{16,0},{1,17},{17,1},{2,18},{18,2},{3,19},{19,3},{4,20},{20... | collective-permute-start | bytes 1572872 | tf_op jit(solution)/shard_map/ppermute | solution.py:30
  49.9 0.0 copy-done.4
  49.9 0.7 fusion.44
  52.6 0.0 copy-done.3
  52.6 0.5 convolution_bitcast_fusion.1
  53.1 6.8 %collective-permute-done.2 = bf16[2,256,512]{2,1,0:T(8,128)(2,1)S(1)} collective-permute-done((bf16[2,256,512]{2,1,0:T(8,128)(2,1)S(1)}, bf16[2,256,512]{2,1,0:T(8,128)(2,1)S(1)}, u32[]{:S(2)}, u32[]{:S(2)}) %collective-permute-start.2) | collective-permute-done | bytes 524320 | tf_op jit(solution)/shard_map/ppermute | solution.py:30
  59.9 0.5 convolution_bitcast_fusion
  60.3 8.0 %fusion.22 = (f32[1,512,512]{1,2,0:T(8,128)S(1)}, f32[1,512,512]{1,2,0:T(8,128)S(1)}, f32[1,512,512]{1,2,0:T(8,128)S(1)}, f32[1,512,512]{1,2,0:T(8,128)S(1)}) fusion(f32[2,512,512]{1,2,0:T(8,128)S(1)} %convolution_bitcast_fusion, f32[512]{0:T(512)S(1)} %get-tuple-element.19, f32[512]{0:T(512)S(1)} %get-tuple-element.18, ...), kind=kLoop, calls=%fused_computation.33 | loop fusion | flops 3670016 | bytes 8394752 | tf_op jit(solution)/shard_map/sub | solution.py:55
  68.4 0.5 maximum_add_fusion
  68.9 1.8 %copy.33 = f32[2,512,512]{2,1,0:T(8,128)} copy(f32[2,512,512]{1,2,0:T(8,128)S(1)} %maximum_add_fusion) | data formatting | bytes 4194304 | tf_op jit(solution)/shard_map/add | solution.py:111
  (5 shorter events, 0.1 us)
Async XLA Ops:
  0.0 44.3 %copy-start = (bf16[1,544,512]{2,1,0:T(8,128)(2,1)S(1)}, bf16[1,544,512]{2,1,0:T(8,128)(2,1)}, u32[]{:S(2)}) copy-start(bf16[1,544,512]{2,1,0:T(8,128)(2,1)} %param.10) | copy-start | bytes 1671172
  0.0 8.7 %copy-start.5 = (s32[1,2,1]{1,2,0:T(1,128)S(1)}, s32[1,2,1]{1,2,0:T(1,128)}, u32[]{:S(2)}) copy-start(s32[1,2,1]{1,2,0:T(1,128)} %param.8) | copy-start | bytes 28
  2.4 31.0 %all-to-all-start = ((bf16[2,32,16,512]{3,1,0,2:T(8,128)(2,1)}), bf16[2,32,16,512]{3,1,0,2:T(8,128)(2,1)S(1)}, u32[]{:S(2)}, u32[]{:S(2)}) async-start(bf16[2,32,16,512]{3,1,0,2:T(8,128)(2,1)} %bitcast.42), calls=%async_computation | async-start | bytes 2097152 | tf_op jit(solution)/shard_map/all_to_all | solution.py:71
  33.4 1.0 %copy-start.1 = (bf16[512,512]{1,0:T(8,128)(2,1)S(1)}, bf16[512,512]{1,0:T(8,128)(2,1)}, u32[]{:S(2)}) copy-start(bf16[512,512]{1,0:T(8,128)(2,1)} %get-tuple-element.16) | copy-start | bytes 1572868
  33.4 1.2 %copy-start.2 = (bf16[512,512]{1,0:T(8,128)(2,1)S(1)}, bf16[512,512]{1,0:T(8,128)(2,1)}, u32[]{:S(2)}) copy-start(bf16[512,512]{1,0:T(8,128)(2,1)} %get-tuple-element.17) | copy-start | bytes 1572868
  35.8 4.9 %copy-start.6 = (s32[1,2,1]{1,2,0:T(1,128)S(1)}, s32[1,2,1]{1,2,0:T(1,128)}, u32[]{:S(2)}) copy-start(s32[1,2,1]{1,2,0:T(1,128)} %param.7) | copy-start | bytes 28
  36.4 5.7 %collective-permute-start.1 = (bf16[2,512,32]{1,2,0:T(8,128)(2,1)S(1)}, bf16[2,512,32]{1,2,0:T(8,128)(2,1)S(1)}, u32[]{:S(2)}, u32[]{:S(2)}) collective-permute-start(bf16[2,512,32]{1,2,0:T(8,128)(2,1)S(1)} %get-tuple-element.11), channel_id=1, source_target_pairs={{1,0},{2,1},{3,2},{4,3},{5,4},{6,5},{7,6},{8,7},{9,8},{10,9},{11,1... | collective-permute-start | bytes 196616 | tf_op jit(solution)/shard_map/ppermute | solution.py:22
  38.8 5.6 %collective-permute-start = (bf16[2,512,32]{1,2,0:T(8,128)(2,1)S(1)}, bf16[2,512,32]{1,2,0:T(8,128)(2,1)S(1)}, u32[]{:S(2)}, u32[]{:S(2)}) collective-permute-start(bf16[2,512,32]{1,2,0:T(8,128)(2,1)S(1)} %get-tuple-element.12), channel_id=1, source_target_pairs={{0,1},{1,2},{2,3},{3,4},{4,5},{5,6},{6,7},{7,8},{8,9},{9,10},{10,1... | collective-permute-start | bytes 196616 | tf_op jit(solution)/shard_map/ppermute | solution.py:21
  42.1 7.9 %copy-start.4 = (f32[1,2]{1,0:T(1,128)S(1)}, f32[1,2]{1,0:T(1,128)}, u32[]{:S(2)}) copy-start(f32[1,2]{1,0:T(1,128)} %param.11) | copy-start | bytes 28
  42.1 10.5 %copy-start.3 = (bf16[1,2,512,256]{3,2,1,0:T(8,128)(2,1)S(1)}, bf16[1,2,512,256]{3,2,1,0:T(8,128)(2,1)}, u32[]{:S(2)}) copy-start(bf16[1,2,512,256]{3,2,1,0:T(8,128)(2,1)} %param.9) | copy-start | bytes 1572868
  45.7 14.1 %collective-permute-start.2 = (bf16[2,256,512]{2,1,0:T(8,128)(2,1)S(1)}, bf16[2,256,512]{2,1,0:T(8,128)(2,1)S(1)}, u32[]{:S(2)}, u32[]{:S(2)}) collective-permute-start(bf16[2,256,512]{2,1,0:T(8,128)(2,1)S(1)} %constant_dynamic-slice_fusion), channel_id=1, source_target_pairs={{0,16},{16,0},{1,17},{17,1},{2,18},{18,2},{3,19},{19,3},{4,20},{20... | collective-permute-start | bytes 1572872 | tf_op jit(solution)/shard_map/ppermute | solution.py:30
where the time goes:
time: 71 us; the launch traced here: 70.7 us
  waiting for transfers between devices  26.3 us (37%)
  other arithmetic  16.2 us (23%)
  starting transfers between devices  12.2 us (17%)
  between operations  6.48 us (9%)
  local copies, waits for them, and re-layouts  6.04 us (9%)
  matrix products  3.55 us (5%)
    all_to_all x1, waiting for transfers between devices, on_device(): lax.all_to_all(split_echoes, 'rng', split_axis=2, concat_axis=1, tiled=True)  17.2 us
    sub x1, other arithmetic, phase_turn(): real_part = real_imag[0] * cosine - real_imag[1] * sine_part  8.02 us
    ppermute x1, waiting for transfers between devices, from_partner(): return lax.ppermute(value, axis, pairs)  6.78 us
    all_to_all x1, starting transfers between devices, on_device(): lax.all_to_all(split_echoes, 'rng', split_axis=2, concat_axis=1, tiled=True)  6.24 us
    another operation x1, other arithmetic  5.74 us
    reshape x1, local copies, waits for them, and re-layouts, on_device(): split_echoes = echoes.reshape(2, local_pulses, rng_count, block_bins)  2.41 us
    ppermute x1, starting transfers between devices, padded(): after = lax.ppermute(leading, axis, down)  2.34 us
    ppermute x1, waiting for transfers between devices, padded(): before = lax.ppermute(last, axis, up)  2.25 us
  transfers between devices with their start and end apart: 4, of which 3 were waited for; matrix products, arithmetic and copies ran while one was open for 12% of the time, Pallas kernels for 0%

commit v1 on v0

v1 whole, which is shorter than its diff:
```python
import functools
import math

import jax
import jax.numpy as jnp
from jax import lax
from jax.experimental import pallas as pl
from jax.experimental.pallas import tpu as pltpu
from jax.sharding import PartitionSpec as P

MAX_SHIFT = 16
LANES = 128
MIB = 2**20
VMEM = pl.BlockSpec(memory_space=pltpu.VMEM)
SMEM = pl.BlockSpec(memory_space=pltpu.SMEM)
ANY = pl.BlockSpec(memory_space=pl.ANY)
F32 = jnp.float32
BF16 = jnp.bfloat16


def dot(a, b):
    return jnp.dot(a, b, preferred_element_type=F32)


def params(mib):
    return pltpu.CompilerParams(vmem_limit_bytes=mib * MIB)


def series(square, first, count):
    coefs = [
        (-1) ** i * math.pi ** (2 * i + first) / math.factorial(2 * i + first)
        for i in range(count)
    ]
    total = jnp.full_like(square, coefs[-1])
    for coef in coefs[-2::-1]:
        total = total * square + coef
    return total


def cos_sin_pi(v):
    turns = jnp.floor(v + 0.5)
    rest = v - turns
    sign = 1.0 - 2.0 * (turns - 2.0 * jnp.floor(turns * 0.5))
    square = rest * rest
    return series(square, 0, 8) * sign, series(square, 1, 7) * rest * sign


def rotated(pair, step):
    return pair[0] * step[0] - pair[1] * step[1], pair[0] * step[1] + pair[1] * step[0]


def place_kernel(echoes_ref, direct_same, direct_cross, keep_ref, give_ref, sems):
    me = lax.axis_index("rng")
    chips = keep_ref.shape[0]
    bins = keep_ref.shape[-1]
    outer = bins // 4
    copies = []

    def take(device, target, first, count, at):
        start = pl.multiple_of(device * bins + first, LANES)
        copy = pltpu.make_async_copy(
            echoes_ref.at[:, pl.ds(start, count)], target.at[:, pl.ds(at, count)], sems.at[len(copies)]
        )
        copy.start()
        copies.append(copy)

    for target, flip in ((direct_same, 0), (direct_cross, 1)):
        device = me ^ (chips + flip)
        take(device, target, 0, outer, 0)
        take(device, target, bins - outer, outer, outer)
    for flip, ref in ((1, give_ref), (0, keep_ref)):
        for d in range(chips):
            device = me ^ (2 * d + flip)
            take(device, ref.at[d], 0, outer, 0)
            take(device, ref.at[d], bins - outer, outer, outer)
            take(device, ref.at[d], outer, bins - 2 * outer, 2 * outer)
    for copy in copies:
        copy.wait()


def placed(echoes, chips, bins):
    rows = echoes.shape[0]
    direct = jax.ShapeDtypeStruct((rows, bins // 2), BF16)
    whole = jax.ShapeDtypeStruct((chips, rows, bins), BF16)
    return pl.pallas_call(
        place_kernel,
        out_shape=[direct, direct, whole, whole],
        in_specs=[ANY],
        out_specs=[VMEM] * 4,
        scratch_shapes=[pltpu.SemaphoreType.DMA((4 + 6 * chips,))],
        compiler_params=params(8),
        cost_estimate=pl.CostEstimate(flops=0, bytes_accessed=3 * MIB, transcendentals=0),
    )(echoes)


def join_kernel(picks, after, keep_ref, got_ref, *refs):
    rows = keep_ref.shape[1]
    for (d, first, count), out_ref in zip(picks, refs[after:]):
        out_ref[:rows] = keep_ref[d, :, first : first + count]
        out_ref[rows:] = got_ref[d, :, first : first + count]


def joined(picks, keep, got, after=()):
    rows = keep.shape[1]
    return pl.pallas_call(
        functools.partial(join_kernel, picks, len(after)),
        out_shape=[jax.ShapeDtypeStruct((2 * rows, count), BF16) for _, _, count in picks],
        in_specs=[VMEM] * 2 + [ANY] * len(after),
        out_specs=[VMEM] * len(picks),
        compiler_params=params(8),
        cost_estimate=pl.CostEstimate(flops=0, bytes_accessed=2 * MIB, transcendentals=0),
    )(keep, got, *after)


def exchanged(value, devices, mask):
    return lax.ppermute(value, "rng", [(i, i ^ mask) for i in range(devices)])


def filter_table_kernel(local_pulses, after_ref, filter_ref, cos_ref, sin_ref):
    me = lax.axis_index("rng")
    columns = filter_ref.shape[1]
    angles = filter_ref.shape[0] // 2
    base = cos_ref.shape[0]
    scale = 1.0 / math.sqrt(columns // 2)
    lane = lax.broadcasted_iota(jnp.int32, (8, columns), 1)
    slot = lane // (2 * local_pulses)
    second = lane // local_pulses % 2
    pulse_id = (slot ^ me) * local_pulses + lane % local_pulses
    pulse = pulse_id.astype(F32)
    lag = second.astype(F32) * 0.5
    per_angle = pulse * (1.0 / angles)
    row = lax.broadcasted_iota(jnp.int32, (8, columns), 0)
    for i in range(base // 8):
        twice = (2 * (row + 8 * i) + 1 - angles).astype(F32)
        cosine, sine = cos_sin_pi(twice * per_angle - lag)
        cos_ref[8 * i : 8 * i + 8, :] = cosine * scale
        sin_ref[8 * i : 8 * i + 8, :] = sine * scale
    step = cos_sin_pi(per_angle * (2 * base))
    for j in range(angles // base):
        for i in range(base // 16):
            pair = [], []
            for k in (2 * i, 2 * i + 1):
                here = slice(8 * k, 8 * k + 8)
                now = cos_ref[here, :], sin_ref[here, :]
                pair[0].append(now[0])
                pair[1].append(-now[1])
                if j + 1 < angles // base:
                    cos_ref[here, :], sin_ref[here, :] = rotated(now, step)
            begin = j * base + 16 * i
            filter_ref[begin : begin + 16, :] = jnp.concatenate(pair[0]).astype(BF16)
            begin += angles
            filter_ref[begin : begin + 16, :] = jnp.concatenate(pair[1]).astype(BF16)


def filter_table(angles, local_pulses, after):
    side = 2 * local_pulses * lax.axis_size("rng")
    return pl.pallas_call(
        functools.partial(filter_table_kernel, local_pulses),
        out_shape=jax.ShapeDtypeStruct((2 * angles, side), BF16),
        in_specs=[ANY],
        out_specs=VMEM,
        scratch_shapes=[pltpu.VMEM((64, side), F32)] * 2,
        compiler_params=params(6),
        cost_estimate=pl.CostEstimate(flops=9_000_000, bytes_accessed=4 * MIB, transcendentals=0),
    )(after)


def merge_table_kernel(
    level, stride, flag_ref, offset_ref, shift_ref, range_ref, after_ref, centre_ref, rim_ref, turn_ref
):
    group = lax.axis_index("sub")
    block = lax.axis_index("rng")
    bins = centre_ref.shape[-1]
    angles = turn_ref.shape[-2]
    total_bins = lax.axis_size("rng") * bins
    own_flag = flag_ref[level, group, 0]
    taps = range_ref.shape[1]
    band = (taps - bins) // 2
    rim = MAX_SHIFT + band
    outer = bins // 4
    kernel = range_ref[level]

    def moved(bin_id):
        tap = lax.broadcasted_iota(jnp.int32, (bin_id.shape[0], taps), 1)
        return dot(jnp.where(tap == bin_id, 1.0, 0.0).astype(BF16), kernel).astype(BF16)

    row = lax.broadcasted_iota(jnp.int32, (2 * outer, 1), 0)
    rim_row = lax.broadcasted_iota(jnp.int32, (8 * rim, 1), 0)
    below = rim_row < 4 * rim
    rim_bin = rim_row % rim + jnp.where(below, -rim, bins)
    rim_group = rim_row % (4 * rim) // rim
    rows = 8
    for child in range(2):
        member = group if child == 0 else group ^ stride
        lead = band - offset_ref[level, member, 0]
        ends = jnp.where(row < outer, row, row + (bins - 2 * outer))
        centre_ref[child, : 2 * outer, :] = moved(ends + lead)
        centre_ref[child, 2 * outer :, :] = moved(row + outer + lead)
        for part in range(2):
            wanted = rim_group == 2 * part + own_flag
            rim_ref[child, part] = moved(jnp.where(wanted, rim_bin + lead, -1))

        rate = shift_ref[level, member]
        bin_id = block * bins + lax.broadcasted_iota(jnp.int32, (1, LANES), 1)
        reach = 1.0 + bin_id.astype(F32) * (1.0 / total_bins)

        def turn_rows(i, carry):
            begin = pl.multiple_of(i * rows, rows)
            angle = begin + lax.broadcasted_iota(jnp.int32, (rows, LANES), 0)
            place = ((angle.astype(F32) + 0.5) * (1.0 / angles) - 0.5) * rate
            now = cos_sin_pi(place * reach)
            step = cos_sin_pi(place * (LANES / total_bins))
            for tile in range(bins // LANES):
                lanes = slice(tile * LANES, tile * LANES + LANES)
                turn_ref[child, 0, pl.ds(begin, rows), lanes] = now[0]
                turn_ref[child, 1, pl.ds(begin, rows), lanes] = now[1]
                now = rotated(now, step)
            return carry

        lax.fori_loop(0, angles // rows, turn_rows, 0, unroll=4)


def merge_tables(level, stride, fore_flag, band_offset, center_shift, range_kernel, angles, after):
    taps, bins = range_kernel.shape[1:]
    rim = MAX_SHIFT + (taps - bins) // 2
    return pl.pallas_call(
        functools.partial(merge_table_kernel, level, stride),
        out_shape=[
            jax.ShapeDtypeStruct((2, bins, bins), BF16),
            jax.ShapeDtypeStruct((2, 2, 8 * rim, bins), BF16),
            jax.ShapeDtypeStruct((2, 2, angles, bins), F32),
        ],
        in_specs=[SMEM] * 3 + [VMEM, ANY],
        out_specs=[VMEM] * 3,
        compiler_params=params(12),
        cost_estimate=pl.CostEstimate(
            flops=2_300_000_000, bytes_accessed=7 * MIB, transcendentals=0
        ),
    )(fore_flag, band_offset, center_shift, range_kernel, after)


def filter_kernel(pieces, first, count, ends, flag_ref, filter_ref, *refs):
    own_flag = flag_ref[0, lax.axis_index("sub"), 0]
    pulses_ref = refs[-1]
    own_ref, out_ref = refs[pieces : pieces + 2]
    at = 0
    for ref in refs[:pieces]:
        begin = first if ref.shape[1] > count else 0
        pulses_ref[at : at + ref.shape[0], :] = ref[:, begin : begin + count]
        at += ref.shape[0]
    half = own_ref.shape[1]
    foremost = own_flag == 0
    edges = [0.0, 0.0]
    for part in range(2):
        pair = []
        for side in range(2):
            begin = (2 * part + side) * half
            image = dot(filter_ref[begin : begin + half, :], pulses_ref[...])
            pair.append(image)
            if ends:
                rim = LANES // 4
                group = 2 * part + side
                lane = lax.broadcasted_iota(jnp.int32, (1, LANES), 1)
                here = lane // rim == group
                low, high = image[:, :LANES], image[:, -LANES:]
                low = pltpu.roll(low, group * rim, 1) if group else low
                turn = (group * rim + rim) % LANES
                high = pltpu.roll(high, turn, 1) if turn else high
                edges[0] = edges[0] + jnp.where(here, low, 0.0)
                edges[1] = edges[1] + jnp.where(here, high, 0.0)
        own_ref[part] = jnp.where(foremost, pair[0], pair[1]).astype(BF16)
        out_ref[part] = jnp.where(foremost, pair[1], pair[0]).astype(BF16)
    if ends:
        refs[pieces + 2][...] = edges[0].astype(BF16)
        refs[pieces + 3][...] = edges[1].astype(BF16)


def filtered(fore_flag, filter_matrix, pieces, first, count, ends):
    half = filter_matrix.shape[0] // 4
    shapes = [jax.ShapeDtypeStruct((2, half, count), BF16)] * 2
    if ends:
        shapes += [jax.ShapeDtypeStruct((half, LANES), BF16)] * 2
    return pl.pallas_call(
        functools.partial(filter_kernel, len(pieces), first, count, ends),
        out_shape=shapes,
        in_specs=[SMEM] + [VMEM] * (1 + len(pieces)),
        out_specs=[VMEM] * len(shapes),
        scratch_shapes=[pltpu.VMEM((filter_matrix.shape[1], count), BF16)],
        compiler_params=params(10),
        cost_estimate=pl.CostEstimate(
            flops=2 * filter_matrix.size * count, bytes_accessed=4 * MIB, transcendentals=0
        ),
    )(fore_flag, filter_matrix, *pieces)


def early_kernel(
    level, flag_ref, own_outer, own_inner, rim_low, rim_high, far_outer, far_low, far_high,
    centre_ref, rim_ref, matrix_ref, turn_ref, merged_ref, partial_ref,
):
    own_flag = flag_ref[level, lax.axis_index("sub"), 0]
    count = own_outer.shape[-1]
    matrix = matrix_ref[level, own_flag]
    rims = jnp.concatenate([rim_low[...], rim_high[...]], axis=1)
    far_rims = jnp.concatenate([far_low[...], far_high[...]], axis=1)
    rows = []
    for part in range(2):
        value = dot(own_outer[part], centre_ref[0, :count, :])
        value += dot(own_inner[part], centre_ref[0, count:, :])
        value += dot(rims, rim_ref[0, part])
        rows.append(value.astype(BF16))
    block = LANES
    for begin in range(0, matrix.shape[0], block):
        here = slice(begin, begin + block)
        real, imag = dot(matrix[here], rows[0]), dot(matrix[here], rows[1])
        merged_ref[0, here], merged_ref[1, here] = rotated(
            (real, imag), (turn_ref[0, 0, here], turn_ref[0, 1, here])
        )
    for part in range(2):
        value = dot(far_outer[part], centre_ref[1, :count, :])
        partial_ref[part] = value + dot(far_rims, rim_ref[1, part])


def late_kernel(
    level, flag_ref, far_inner, merged_ref, partial_ref, centre_ref, matrix_ref, turn_ref, out_ref,
    buffer, sems,
):
    own_flag = flag_ref[level, lax.axis_index("sub"), 0]
    count = far_inner.shape[-1]
    matrix = matrix_ref[level, 1 - own_flag]
    rows = []
    for part in range(2):
        value = partial_ref[part] + dot(far_inner[part], centre_ref[1, count:, :])
        rows.append(value.astype(BF16))
    block = LANES
    copies = []
    for begin in range(0, matrix.shape[0], block):
        here = slice(begin, begin + block)
        real, imag = dot(matrix[here], rows[0]), dot(matrix[here], rows[1])
        real, imag = rotated((real, imag), (turn_ref[1, 0, here], turn_ref[1, 1, here]))
        buffer[0, here] = (merged_ref[0, here] + real).astype(buffer.dtype)
        buffer[1, here] = (merged_ref[1, here] + imag).astype(buffer.dtype)
        copy = pltpu.make_async_copy(
            buffer.at[:, here], out_ref.at[:, here], sems.at[begin // block]
        )
        copy.start()
        copies.append(copy)
    for copy in copies:
        copy.wait()


def merged_image(level, fore_flag, own, rims, far, far_rims, centre, rim, angle_interp, turn, dtype):
    angles, bins = turn.shape[-2:]
    cost = pl.CostEstimate(flops=4 * angles * bins * bins, bytes_accessed=8 * MIB, transcendentals=0)
    merged, partial = pl.pallas_call(
        functools.partial(early_kernel, level),
        out_shape=[
            jax.ShapeDtypeStruct((2, angles, bins), F32),
            jax.ShapeDtypeStruct((2, angles // 2, bins), F32),
        ],
        in_specs=[SMEM] + [VMEM] * 11,
        out_specs=[VMEM] * 2,
        compiler_params=params(20),
        cost_estimate=cost,
    )(fore_flag, *own, *rims, far[0], *far_rims, centre, rim, angle_interp, turn)
    return pl.pallas_call(
        functools.partial(late_kernel, level),
        out_shape=jax.ShapeDtypeStruct((2, angles, bins), dtype),
        in_specs=[SMEM] + [VMEM] * 6,
        out_specs=ANY,
        scratch_shapes=[
            pltpu.VMEM((2, angles, bins), dtype),
            pltpu.SemaphoreType.DMA((angles // LANES,)),
        ],
        compiler_params=params(20),
        cost_estimate=cost,
    )(fore_flag, far[1], merged, partial, centre, angle_interp, turn)


def neighbour_rims(low, high):
    devices = lax.axis_size("rng")
    up = [(i, i + 1) for i in range(devices - 1)]
    below = lax.ppermute(high, "rng", up)
    above = lax.ppermute(low, "rng", [(j, i) for i, j in up])
    return below, above


def from_partner(value, stride):
    pairs = [(source, source ^ stride) for source in range(lax.axis_size("sub"))]
    return lax.ppermute(value, "sub", pairs)


def split_image(level, image, fore_flag, rim):
    angles, bins = image.shape[1:]
    half, outer = angles // 2, bins // 4
    own_flag = fore_flag[level, lax.axis_index("sub"), 0]
    sides = image.reshape(2, 2, half, bins)

    def pieces(side):
        rows = lax.dynamic_index_in_dim(sides, side, 1, keepdims=False)
        ends = jnp.concatenate([rows[..., :outer], rows[..., -outer:]], axis=-1)
        return ends, rows[..., outer:-outer]

    def packed(edge):
        return edge.transpose(2, 0, 1, 3).reshape(half, 4 * rim)

    low, high = packed(sides[..., :rim]), packed(sides[..., -rim:])
    return pieces(own_flag), pieces(1 - own_flag), low, high


def on_device(echoes, fore_flag, band_offset, angle_interp, range_kernel, center_shift):
    devices = lax.axis_size("rng")
    chips = devices // 2
    far_chip = chips // 2
    local_pulses = echoes.shape[1]
    bins = echoes.shape[2] // devices
    count = bins // 2
    angles = angle_interp.shape[2]
    rim = MAX_SHIFT + (range_kernel.shape[1] - bins) // 2
    levels = range_kernel.shape[0]

    rows = echoes.reshape(2 * local_pulses, devices * bins)
    direct_same, direct_cross, keep, give = placed(rows, chips, bins)
    direct = (
        exchanged(direct_same, devices, chips),
        exchanged(direct_cross, devices, chips + 1),
    )
    got = exchanged(give, devices, 1)
    first_far = range(far_chip + 1, chips)
    near = range(1, far_chip)
    picks = [(d, 0, count) for d in first_far] + [(d, 0, bins) for d in (*near, 0)]
    sends = joined(picks, keep, got)
    outer_far = [
        exchanged(value, devices, 2 * d) for d, value in zip(first_far, sends)
    ]
    whole = [sends[-1]] + [
        exchanged(value, devices, 2 * d) for d, value in zip(near, sends[len(first_far) :])
    ]
    later = range(far_chip, chips)
    late_sends = joined([(d, count, count) for d in later], keep, got, (outer_far[0],))
    inner_far = [exchanged(value, devices, 2 * d) for d, value in zip(later, late_sends)]

    filter_matrix = filter_table(angles, local_pulses, sends[-1])
    settings = (fore_flag, band_offset, center_shift, range_kernel, angles)
    centre, rim_matrix, turn = merge_tables(0, 1, *settings, filter_matrix)

    own_outer, out_outer, low, high = filtered(
        fore_flag, filter_matrix, (*whole, *direct, *outer_far), 0, count, True
    )
    rims = neighbour_rims(low, high)
    far_outer = from_partner(out_outer, 1)
    far_rims = [from_partner(value, 1) for value in rims]
    own_inner, out_inner = filtered(
        fore_flag, filter_matrix, (*whole, *inner_far), count, count, False
    )
    far_inner = from_partner(out_inner, 1)
    own, far = (own_outer, own_inner), (far_outer, far_inner)
    for level in range(levels):
        if level > 0:
            stride = 2**level
            centre, rim_matrix, turn = merge_tables(level, stride, *settings, image)
            own, out, low, high = split_image(level, image, fore_flag, rim)
            rims = neighbour_rims(low, high)
            far = [from_partner(value, stride) for value in out]
            far_rims = [from_partner(value, stride) for value in rims]
        dtype = BF16 if level + 1 < levels else F32
        image = merged_image(
            level, fore_flag, own, rims, far, far_rims, centre, rim_matrix, angle_interp, turn, dtype
        )
    return image


def solution(mesh):
    placed_as = (
        P(None, ("sub", "rng"), None),
        P(None, None, "rng"),
        P(None, None, "rng"),
        P(),
        P(),
        P(),
    )
    return jax.shard_map(
        on_device, mesh=mesh, in_specs=placed_as, out_specs=P(None, "sub", "rng"), check_vma=False
    )
```

time: 71 us -> 61.4 us (0.86)
  the two profiles are of different devices: /device:TPU:10 before, /device:TPU:6 now
where the time goes in v1:
time: 61.4 us; the launch traced here: 61.2 us
  starting transfers between devices  29.4 us (48%)
  Pallas kernels  15.9 us (26%)
  waiting for transfers between devices  13.6 us (22%)
  local copies, waits for them, and re-layouts  2.15 us (4%)
    ppermute x13, starting transfers between devices, exchanged(): return lax.ppermute(value, 'rng', [(i, i ^ mask) for i in range(devices)])  19.5 us
    ppermute x13, waiting for transfers between devices, exchanged(): return lax.ppermute(value, 'rng', [(i, i ^ mask) for i in range(devices)])  7.72 us
    ppermute x4, waiting for transfers between devices, from_partner(): return lax.ppermute(value, 'sub', pairs)  5.9 us
    pallas_call x1, Pallas kernels, merge_tables(): pl.pallas_call(functools.partial(merge_table_kernel, level, stride), out_...  4.8 us
    ppermute x4, starting transfers between devices, from_partner(): return lax.ppermute(value, 'sub', pairs)  4.15 us
    ppermute x1, starting transfers between devices, neighbour_rims(): above = lax.ppermute(low, 'rng', [(j, i) for i, j in up])  3.64 us
    pallas_call x2, Pallas kernels, filtered(): pl.pallas_call(functools.partial(filter_kernel, len(pieces), first, count...  3.27 us
    pallas_call x1, Pallas kernels, merged_image(): pl.pallas_call(functools.partial(late_kernel, level), out_shape=jax.Shape...  2.53 us
  transfers between devices with their start and end apart: 19, of which 4 were waited for; matrix products, arithmetic and copies ran while one was open for 0% of the time, Pallas kernels for 20%

profile of v1, /device:TPU:6, one launch (start us, length us, event | category | flops | bytes accessed | tf_op | source)
XLA Modules:
  0.0 61.2 jit_solution(1651534140118244268)
XLA Ops:
  0.0 0.0 copy-start.5
  0.0 0.0 copy-start.1
  0.0 1.2 %copy-done.1 = bf16[2,32,8192]{2,1,0:T(8,128)(2,1)S(1)} copy-done((bf16[2,32,8192]{2,1,0:T(8,128)(2,1)S(1)}, bf16[2,32,8192]{2,1,0:T(8,128)(2,1)}, u32[]{:S(2)}) %copy-start.1) | copy-done | bytes 1048600
  1.2 0.9 %shard_map.64 = (bf16[64,256]{1,0:T(8,128)(2,1)S(1)}, bf16[64,256]{1,0:T(8,128)(2,1)S(1)}, bf16[8,64,512]{2,1,0:T(8,128)(2,1)S(1)}, bf16[8,64,512]{2,1,0:T(8,128)(2,1)S(1)}) custom-call(bf16[64,8192]{1,0:T(8,128)(2,1)S(1)} %bitcast.1), custom_call_target="tpu_custom_call" | custom-call | bytes 3145728 | tf_op jit(solution)/shard_map/pallas_call | solution.py:85
  2.2 0.1 collective-permute-start
  2.2 2.7 %collective-permute-start.10 = (bf16[64,256]{1,0:T(8,128)(2,1)S(1)}, bf16[64,256]{1,0:T(8,128)(2,1)S(1)}, u32[]{:S(2)}, u32[]{:S(2)}) collective-permute-start(bf16[64,256]{1,0:T(8,128)(2,1)S(1)} %get-tuple-element.43), channel_id=1, source_target_pairs={{0,8},{1,9},{2,10},{3,11},{4,12},{5,13},{6,14},{7,15},{8,0},{9,1},... | collective-permute-start | bytes 98312 | tf_op jit(solution)/shard_map/ppermute | solution.py:116
  4.9 0.0 collective-permute-done.got_ref
  4.9 0.7 %shard_map.65 = (bf16[128,256]{1,0:T(8,128)(2,1)S(1)}, bf16[128,256]{1,0:T(8,128)(2,1)S(1)}, bf16[128,256]{1,0:T(8,128)(2,1)}, bf16[128,512]{1,0:T(8,128)(2,1)S(...) custom-call(bf16[8,64,512]{2,1,0:T(8,128)(2,1)S(1)} %get-tuple-element.31.keep_ref, ...), custom_call_target="tpu_custom_call" | custom-call | bytes 2097152 | tf_op jit(solution)/shard_map/pallas_call | solution.py:105
  5.6 1.8 %collective-permute-start.4 = (bf16[128,256]{1,0:T(8,128)(2,1)S(1)}, bf16[128,256]{1,0:T(8,128)(2,1)S(1)}, u32[]{:S(2)}, u32[]{:S(2)}) collective-permute-start(bf16[128,256]{1,0:T(8,128)(2,1)S(1)} %get-tuple-element.37), channel_id=1, source_target_pairs={{0,10},{1,11},{2,8},{3,9},{4,14},{5,15},{6,12},{7,13},{8,2},{9,3},... | collective-permute-start | bytes 196616 | tf_op jit(solution)/shard_map/ppermute | solution.py:116
  7.4 1.5 %collective-permute-start.1 = (bf16[128,512]{1,0:T(8,128)(2,1)S(1)}, bf16[128,512]{1,0:T(8,128)(2,1)S(1)}, u32[]{:S(2)}, u32[]{:S(2)}) collective-permute-start(bf16[128,512]{1,0:T(8,128)(2,1)S(1)} %get-tuple-element.34), channel_id=1, source_target_pairs={{0,2},{1,3},{2,0},{3,1},{4,6},{5,7},{6,4},{7,5},{8,10},{9,11},{10,... | collective-permute-start | bytes 393224 | tf_op jit(solution)/shard_map/ppermute | solution.py:116
  8.9 1.6 %collective-permute-start.2 = (bf16[128,512]{1,0:T(8,128)(2,1)S(1)}, bf16[128,512]{1,0:T(8,128)(2,1)S(1)}, u32[]{:S(2)}, u32[]{:S(2)}) collective-permute-start(bf16[128,512]{1,0:T(8,128)(2,1)S(1)} %get-tuple-element.35), channel_id=1, source_target_pairs={{0,4},{1,5},{2,6},{3,7},{4,0},{5,1},{6,2},{7,3},{8,12},{9,13},{10,... | collective-permute-start | bytes 393224 | tf_op jit(solution)/shard_map/ppermute | solution.py:116
  10.4 0.4 collective-permute-start.3
  10.9 0.0 collective-permute-done.10.refs_4_
  10.9 0.0 collective-permute-start.11
  10.9 5.6 %collective-permute-done.11.refs_5_ = bf16[64,256]{1,0:T(8,128)(2,1)S(1)} collective-permute-done((bf16[64,256]{1,0:T(8,128)(2,1)S(1)}, bf16[64,256]{1,0:T(8,128)(2,1)S(1)}, u32[]{:S(2)}, u32[]{:S(2)}) %collective-permute-start.11) | collective-permute-done | bytes 32800 | tf_op jit(solution)/shard_map/ppermute | solution.py:116
  16.5 1.1 %collective-permute-start.12 = (bf16[128,256]{1,0:T(8,128)(2,1)S(1)}, bf16[128,256]{1,0:T(8,128)(2,1)S(1)}, u32[]{:S(2)}, u32[]{:S(2)}) collective-permute-start(bf16[128,256]{1,0:T(8,128)(2,1)S(1)} %get-tuple-element.45), channel_id=1, source_target_pairs={{0,12},{1,13},{2,14},{3,15},{4,8},{5,9},{6,10},{7,11},{8,4},{9,5},... | collective-permute-start | bytes 196616 | tf_op jit(solution)/shard_map/ppermute | solution.py:116
  17.6 0.0 collective-permute-done.4.refs_0_.refs_6_
  17.6 2.7 %collective-permute-start.13 = (bf16[128,256]{1,0:T(8,128)(2,1)}, bf16[128,256]{1,0:T(8,128)(2,1)S(1)}, u32[]{:S(2)}, u32[]{:S(2)}) collective-permute-start(bf16[128,256]{1,0:T(8,128)(2,1)} %get-tuple-element.46), channel_id=1, source_target_pairs={{0,14},{1,15},{2,12},{3,13},{4,10},{5,11},{6,8},{7,9},{8,6},{9,7},... | collective-permute-start | bytes 196616 | tf_op jit(solution)/shard_map/ppermute | solution.py:116
  20.3 0.7 %shard_map.67 = (bf16[128,256]{1,0:T(8,128)(2,1)}, bf16[128,256]{1,0:T(8,128)(2,1)}, bf16[128,256]{1,0:T(8,128)(2,1)S(1)}, bf16[128,256]{1,0:T(8,128)(2,1)S(1)}) custom-call(bf16[8,64,512]{2,1,0:T(8,128)(2,1)S(1)} %get-tuple-element.31.keep_ref, bf16[8,64,512]{2,1,0:T(8,128)(2,1)S(1)} %collective-permute-done.got_ref, ...), custom_call_target="tpu_custom_call" | custom-call | bytes 2097152 | tf_op jit(solution)/shard_map/pallas_call | solution.py:105
  20.9 2.1 %collective-permute-done.12.refs_7_ = bf16[128,256]{1,0:T(8,128)(2,1)S(1)} collective-permute-done((bf16[128,256]{1,0:T(8,128)(2,1)S(1)}, bf16[128,256]{1,0:T(8,128)(2,1)S(1)}, u32[]{:S(2)}, u32[]{:S(2)}) %collective-permute-start.12) | collective-permute-done | bytes 65568 | tf_op jit(solution)/shard_map/ppermute | solution.py:116
  23.0 1.5 %collective-permute-start.5 = (bf16[128,256]{1,0:T(8,128)(2,1)}, bf16[128,256]{1,0:T(8,128)(2,1)S(1)}, u32[]{:S(2)}, u32[]{:S(2)}) collective-permute-start(bf16[128,256]{1,0:T(8,128)(2,1)} %get-tuple-element.38), channel_id=1, source_target_pairs={{0,8},{1,9},{2,10},{3,11},{4,12},{5,13},{6,14},{7,15},{8,0},{9,1},... | collective-permute-start | bytes 196616 | tf_op jit(solution)/shard_map/ppermute | solution.py:116
  24.5 0.0 copy-done.5
  24.5 0.1 copy.12.flag_ref
  24.6 0.0 copy-start.6
  24.6 1.0 %shard_map.66.filter_ref.after_ref = bf16[1024,1024]{1,0:T(8,128)(2,1)S(1)} custom-call(bf16[128,512]{1,0:T(8,128)(2,1)S(1)} %get-tuple-element.33.after_ref.refs_0_), custom_call_target="tpu_custom_call" | custom-call | flops 9000000 | bytes 4194304 | tf_op jit(solution)/shard_map/pallas_call | solution.py:157
  25.6 0.0 collective-permute-done.13.refs_8_
  25.6 1.9 %collective-permute-start.6 = (bf16[128,256]{1,0:T(8,128)(2,1)}, bf16[128,256]{1,0:T(8,128)(2,1)S(1)}, u32[]{:S(2)}, u32[]{:S(2)}) collective-permute-start(bf16[128,256]{1,0:T(8,128)(2,1)} %get-tuple-element.39), channel_id=1, source_target_pairs={{0,10},{1,11},{2,8},{3,9},{4,14},{5,15},{6,12},{7,13},{8,2},{9,3},... | collective-permute-start | bytes 196616 | tf_op jit(solution)/shard_map/ppermute | solution.py:116
  27.5 0.0 collective-permute-done.1.refs_1_
  27.5 1.7 %collective-permute-start.7 = (bf16[128,256]{1,0:T(8,128)(2,1)S(1)}, bf16[128,256]{1,0:T(8,128)(2,1)S(1)}, u32[]{:S(2)}, u32[]{:S(2)}) collective-permute-start(bf16[128,256]{1,0:T(8,128)(2,1)S(1)} %get-tuple-element.40), channel_id=1, source_target_pairs={{0,12},{1,13},{2,14},{3,15},{4,8},{5,9},{6,10},{7,11},{8,4},{9,5},... | collective-permute-start | bytes 196616 | tf_op jit(solution)/shard_map/ppermute | solution.py:116
  29.3 0.0 collective-permute-done.2.refs_2_
  29.3 2.6 %collective-permute-start.8 = (bf16[128,256]{1,0:T(8,128)(2,1)S(1)}, bf16[128,256]{1,0:T(8,128)(2,1)S(1)}, u32[]{:S(2)}, u32[]{:S(2)}) collective-permute-start(bf16[128,256]{1,0:T(8,128)(2,1)S(1)} %get-tuple-element.41), channel_id=1, source_target_pairs={{0,14},{1,15},{2,12},{3,13},{4,10},{5,11},{6,8},{7,9},{8,6},{9,7},... | collective-permute-start | bytes 196616 | tf_op jit(solution)/shard_map/ppermute | solution.py:116
  31.9 0.0 collective-permute-done.3.refs_3_
  31.9 2.0 %shard_map.69 = (bf16[2,256,256]{2,1,0:T(8,128)(2,1)S(1)}, bf16[2,256,256]{2,1,0:T(8,128)(2,1)S(1)}, bf16[256,128]{1,0:T(8,128)(2,1)}, bf16[256,128]{1,0:T(8,128)(2,1)}) custom-call(s32[1,2,1]{2,1,0:T(2,128)S(1)} %copy.12.flag_ref, bf16[1024,1024]{1,0:T(8,128)(2,1)S(1)} %shard_map.66.filter_ref.after_ref, ...), custom_call_target="tpu_custom_call" | custom-call | flops 536870912 | bytes 4194304 | tf_op jit(solution)/shard_map/pallas_call | solution.py:283
  33.9 0.0 copy-start.3
  33.9 0.7 %copy-done.3 = bf16[2,256,256]{2,1,0:T(8,128)(2,1)} copy-done((bf16[2,256,256]{2,1,0:T(8,128)(2,1)}, bf16[2,256,256]{2,1,0:T(8,128)(2,1)S(1)}, u32[]{:S(2)}) %copy-start.3) | copy-done | bytes 262168
  34.6 0.0 copy-start.4
  34.6 2.0 %collective-permute-start.14 = (bf16[256,128]{1,0:T(8,128)(2,1)}, bf16[256,128]{1,0:T(8,128)(2,1)S(1)}, u32[]{:S(2)}, u32[]{:S(2)}) collective-permute-start(bf16[256,128]{1,0:T(8,128)(2,1)} %get-tuple-element.49), channel_id=1, source_target_pairs={{0,1},{1,2},{2,3},{3,4},{4,5},{5,6},{6,7},{7,8},{8,9},{9,10},{10,1... | collective-permute-start | bytes 196616 | tf_op jit(solution)/shard_map/ppermute | solution.py:382
  36.6 0.0 collective-permute-done.5.refs_4_
  36.6 3.6 %collective-permute-start.15 = (bf16[256,128]{1,0:T(8,128)(2,1)}, bf16[256,128]{1,0:T(8,128)(2,1)S(1)}, u32[]{:S(2)}, u32[]{:S(2)}) collective-permute-start(bf16[256,128]{1,0:T(8,128)(2,1)} %get-tuple-element.50), channel_id=1, source_target_pairs={{1,0},{2,1},{3,2},{4,3},{5,4},{6,5},{7,6},{8,7},{9,8},{10,9},{11,1... | collective-permute-start | bytes 196616 | tf_op jit(solution)/shard_map/ppermute | solution.py:383
  40.3 0.0 copy-done.6
  40.3 0.1 copy.10.offset_ref
  40.4 0.0 copy-start.2
  40.4 0.0 collective-permute-done.6.refs_5_
  40.4 0.5 collective-permute-start.16
  40.9 0.0 collective-permute-done.7.refs_6_
  40.9 0.0 collective-permute-done.8.refs_7_
  40.9 1.3 %shard_map.68 = (bf16[2,256,256]{2,1,0:T(8,128)(2,1)S(1)}, bf16[2,256,256]{2,1,0:T(8,128)(2,1)S(1)}) custom-call(s32[1,2,1]{2,1,0:T(2,128)S(1)} %copy.12.flag_ref, bf16[1024,1024]{1,0:T(8,128)(2,1)S(1)} %shard_map.66.filter_ref.after_ref, bf16[128,512]{1,0:T(8,128)(2,1)S(1)} %get-tuple-element.33.after_ref.refs_0_, ...), custom_call_target="tpu_custom_call" | custom-call | flops 536870912 | bytes 4194304 | tf_op jit(solution)/shard_map/pallas_call | solution.py:283
  42.2 0.0 copy-start
  42.2 1.6 %collective-permute-start.9 = (bf16[2,256,256]{2,1,0:T(8,128)(2,1)S(1)}, bf16[2,256,256]{2,1,0:T(8,128)(2,1)S(1)}, u32[]{:S(2)}, u32[]{:S(2)}) collective-permute-start(bf16[2,256,256]{2,1,0:T(8,128)(2,1)S(1)} %get-tuple-element.42), channel_id=1, source_target_pairs={{0,16},{16,0},{1,17},{17,1},{2,18},{18,2},{3,19},{19,3},{4,20},{20... | collective-permute-start | bytes 786440 | tf_op jit(solution)/shard_map/ppermute | solution.py:389
  43.8 0.0 collective-permute-done.14.rim_low
  43.8 0.5 collective-permute-start.17
  44.3 0.0 collective-permute-done.15.rim_high
  44.3 1.5 %collective-permute-start.18 = (bf16[256,128]{1,0:T(8,128)(2,1)S(1)}, bf16[256,128]{1,0:T(8,128)(2,1)S(1)}, u32[]{:S(2)}, u32[]{:S(2)}) collective-permute-start(bf16[256,128]{1,0:T(8,128)(2,1)S(1)} %collective-permute-done.15.rim_high), channel_id=1, source_target_pairs={{0,16},{16,0},{1,17},{17,1},{2,18},{18,2},{3,19},{19,3},{4,20},{20... | collective-permute-start | bytes 196616 | tf_op jit(solution)/shard_map/ppermute | solution.py:389
  45.8 0.0 copy-done.4
  45.8 0.0 copy-done.2
  45.8 4.8 %shard_map.70 = (bf16[2,512,512]{2,1,0:T(8,128)(2,1)S(1)}, bf16[2,2,256,512]{3,2,1,0:T(8,128)(2,1)S(1)}, f32[2,2,512,512]{3,2,1,0:T(8,128)S(1)}) custom-call(s32[1,2,1]{2,1,0:T(2,128)S(1)} %copy.12.flag_ref, s32[1,2,1]{2,1,0:T(2,128)S(1)} %copy.10.offset_ref, f32[1,2]{1,0:T(1,128)S(1)} %copy-done.4, bf16[1,544,512]{2,1,0:T(8,128)(2,1)S(1)} %copy-done.2, ...), custom_call_target="tpu_custom_call" | custom-call | flops 2300000000 | bytes 7340032 | tf_op jit(solution)/shard_map/pallas_call | solution.py:226
  50.6 5.2 %collective-permute-done.17.far_low = bf16[256,128]{1,0:T(8,128)(2,1)S(1)} collective-permute-done((bf16[256,128]{1,0:T(8,128)(2,1)S(1)}, bf16[256,128]{1,0:T(8,128)(2,1)S(1)}, u32[]{:S(2)}, u32[]{:S(2)}) %collective-permute-start.17) | collective-permute-done | bytes 65568 | tf_op jit(solution)/shard_map/ppermute | solution.py:389
  55.8 0.7 %collective-permute-done.18.far_high = bf16[256,128]{1,0:T(8,128)(2,1)S(1)} collective-permute-done((bf16[256,128]{1,0:T(8,128)(2,1)S(1)}, bf16[256,128]{1,0:T(8,128)(2,1)S(1)}, u32[]{:S(2)}, u32[]{:S(2)}) %collective-permute-start.18) | collective-permute-done | bytes 65568 | tf_op jit(solution)/shard_map/ppermute | solution.py:389
  56.5 0.0 collective-permute-done.16.far_outer
  56.6 0.0 copy-done
  56.6 2.1 %shard_map.71 = (f32[2,512,512]{2,1,0:T(8,128)S(1)}, f32[2,256,512]{2,1,0:T(8,128)S(1)}) custom-call(s32[1,2,1]{2,1,0:T(2,128)S(1)} %copy.12.flag_ref, bf16[2,256,256]{2,1,0:T(8,128)(2,1)S(1)} %get-tuple-element.47.own_outer, bf16[2,256,256]{2,1,0:T(8,128)(2,1)S(1)} %get-tuple-element.48.own_inner, bf16[256,128]{1,0:T(8,128)(2,1)S(1)} %collective-permute-done.14.rim_low, ...), custom_call_target="tpu_custom_call" | custom-call | flops 536870912 | bytes 8388608 | tf_op jit(solution)/shard_map/pallas_call | solution.py:354
  58.6 0.0 collective-permute-done.9.far_inner
  58.6 2.5 %shard_map.72 = f32[2,512,512]{2,1,0:T(8,128)} custom-call(s32[1,2,1]{2,1,0:T(2,128)S(1)} %copy.12.flag_ref, bf16[2,256,256]{2,1,0:T(8,128)(2,1)S(1)} %collective-permute-done.9.far_inner, f32[2,512,512]{2,1,0:T(8,128)S(1)} %get-tuple-element.55.merged_ref, f32[2,256,512]{2,1,0:T(8,128)S(1)} %get-tuple-element.56.partial_ref, ...), custom_call_target="tpu_custom_call" | custom-call | flops 536870912 | bytes 8388608 | tf_op jit(solution)/shard_map/pallas_call | solution.py:365
Async XLA Ops:
  0.0 24.5 %copy-start.5 = (s32[1,2,1]{1,2,0:T(1,128)S(1)}, s32[1,2,1]{1,2,0:T(1,128)}, u32[]{:S(2)}) copy-start(s32[1,2,1]{1,2,0:T(1,128)} %param.7) | copy-start | bytes 28
  0.0 1.2 %copy-start.1 = (bf16[2,32,8192]{2,1,0:T(8,128)(2,1)S(1)}, bf16[2,32,8192]{2,1,0:T(8,128)(2,1)}, u32[]{:S(2)}) copy-start(bf16[2,32,8192]{2,1,0:T(8,128)(2,1)} %param.6) | copy-start | bytes 3145732
  2.2 2.7 %collective-permute-start = (bf16[8,64,512]{2,1,0:T(8,128)(2,1)S(1)}, bf16[8,64,512]{2,1,0:T(8,128)(2,1)S(1)}, u32[]{:S(2)}, u32[]{:S(2)}) collective-permute-start(bf16[8,64,512]{2,1,0:T(8,128)(2,1)S(1)} %get-tuple-element.32), channel_id=1, source_target_pairs={{0,1},{1,0},{2,3},{3,2},{4,5},{5,4},{6,7},{7,6},{8,9},{9,8},{10,11... | collective-permute-start | bytes 1572872 | tf_op jit(solution)/shard_map/ppermute | solution.py:116
  2.2 8.6 %collective-permute-start.10 = (bf16[64,256]{1,0:T(8,128)(2,1)S(1)}, bf16[64,256]{1,0:T(8,128)(2,1)S(1)}, u32[]{:S(2)}, u32[]{:S(2)}) collective-permute-start(bf16[64,256]{1,0:T(8,128)(2,1)S(1)} %get-tuple-element.43), channel_id=1, source_target_pairs={{0,8},{1,9},{2,10},{3,11},{4,12},{5,13},{6,14},{7,15},{8,0},{9,1},... | collective-permute-start | bytes 98312 | tf_op jit(solution)/shard_map/ppermute | solution.py:116
  5.6 12.0 %collective-permute-start.4 = (bf16[128,256]{1,0:T(8,128)(2,1)S(1)}, bf16[128,256]{1,0:T(8,128)(2,1)S(1)}, u32[]{:S(2)}, u32[]{:S(2)}) collective-permute-start(bf16[128,256]{1,0:T(8,128)(2,1)S(1)} %get-tuple-element.37), channel_id=1, source_target_pairs={{0,10},{1,11},{2,8},{3,9},{4,14},{5,15},{6,12},{7,13},{8,2},{9,3},... | collective-permute-start | bytes 196616 | tf_op jit(solution)/shard_map/ppermute | solution.py:116
  7.4 20.2 %collective-permute-start.1 = (bf16[128,512]{1,0:T(8,128)(2,1)S(1)}, bf16[128,512]{1,0:T(8,128)(2,1)S(1)}, u32[]{:S(2)}, u32[]{:S(2)}) collective-permute-start(bf16[128,512]{1,0:T(8,128)(2,1)S(1)} %get-tuple-element.34), channel_id=1, source_target_pairs={{0,2},{1,3},{2,0},{3,1},{4,6},{5,7},{6,4},{7,5},{8,10},{9,11},{10,... | collective-permute-start | bytes 393224 | tf_op jit(solution)/shard_map/ppermute | solution.py:116
  8.9 20.4 %collective-permute-start.2 = (bf16[128,512]{1,0:T(8,128)(2,1)S(1)}, bf16[128,512]{1,0:T(8,128)(2,1)S(1)}, u32[]{:S(2)}, u32[]{:S(2)}) collective-permute-start(bf16[128,512]{1,0:T(8,128)(2,1)S(1)} %get-tuple-element.35), channel_id=1, source_target_pairs={{0,4},{1,5},{2,6},{3,7},{4,0},{5,1},{6,2},{7,3},{8,12},{9,13},{10,... | collective-permute-start | bytes 393224 | tf_op jit(solution)/shard_map/ppermute | solution.py:116
  10.4 21.4 %collective-permute-start.3 = (bf16[128,512]{1,0:T(8,128)(2,1)S(1)}, bf16[128,512]{1,0:T(8,128)(2,1)S(1)}, u32[]{:S(2)}, u32[]{:S(2)}) collective-permute-start(bf16[128,512]{1,0:T(8,128)(2,1)S(1)} %get-tuple-element.36), channel_id=1, source_target_pairs={{0,6},{1,7},{2,4},{3,5},{4,2},{5,3},{6,0},{7,1},{8,14},{9,15},{10,... | collective-permute-start | bytes 393224 | tf_op jit(solution)/shard_map/ppermute | solution.py:116
  10.9 5.6 %collective-permute-start.11 = (bf16[64,256]{1,0:T(8,128)(2,1)S(1)}, bf16[64,256]{1,0:T(8,128)(2,1)S(1)}, u32[]{:S(2)}, u32[]{:S(2)}) collective-permute-start(bf16[64,256]{1,0:T(8,128)(2,1)S(1)} %get-tuple-element.44), channel_id=1, source_target_pairs={{0,9},{1,8},{2,11},{3,10},{4,13},{5,12},{6,15},{7,14},{8,1},{9,0},... | collective-permute-start | bytes 98312 | tf_op jit(solution)/shard_map/ppermute | solution.py:116
  16.5 6.6 %collective-permute-start.12 = (bf16[128,256]{1,0:T(8,128)(2,1)S(1)}, bf16[128,256]{1,0:T(8,128)(2,1)S(1)}, u32[]{:S(2)}, u32[]{:S(2)}) collective-permute-start(bf16[128,256]{1,0:T(8,128)(2,1)S(1)} %get-tuple-element.45), channel_id=1, source_target_pairs={{0,12},{1,13},{2,14},{3,15},{4,8},{5,9},{6,10},{7,11},{8,4},{9,5},... | collective-permute-start | bytes 196616 | tf_op jit(solution)/shard_map/ppermute | solution.py:116
  17.6 8.0 %collective-permute-start.13 = (bf16[128,256]{1,0:T(8,128)(2,1)}, bf16[128,256]{1,0:T(8,128)(2,1)S(1)}, u32[]{:S(2)}, u32[]{:S(2)}) collective-permute-start(bf16[128,256]{1,0:T(8,128)(2,1)} %get-tuple-element.46), channel_id=1, source_target_pairs={{0,14},{1,15},{2,12},{3,13},{4,10},{5,11},{6,8},{7,9},{8,6},{9,7},... | collective-permute-start | bytes 196616 | tf_op jit(solution)/shard_map/ppermute | solution.py:116
  23.0 13.6 %collective-permute-start.5 = (bf16[128,256]{1,0:T(8,128)(2,1)}, bf16[128,256]{1,0:T(8,128)(2,1)S(1)}, u32[]{:S(2)}, u32[]{:S(2)}) collective-permute-start(bf16[128,256]{1,0:T(8,128)(2,1)} %get-tuple-element.38), channel_id=1, source_target_pairs={{0,8},{1,9},{2,10},{3,11},{4,12},{5,13},{6,14},{7,15},{8,0},{9,1},... | collective-permute-start | bytes 196616 | tf_op jit(solution)/shard_map/ppermute | solution.py:116
  24.6 15.7 %copy-start.6 = (s32[1,2,1]{1,2,0:T(1,128)S(1)}, s32[1,2,1]{1,2,0:T(1,128)}, u32[]{:S(2)}) copy-start(s32[1,2,1]{1,2,0:T(1,128)} %param.8) | copy-start | bytes 28
  25.6 14.8 %collective-permute-start.6 = (bf16[128,256]{1,0:T(8,128)(2,1)}, bf16[128,256]{1,0:T(8,128)(2,1)S(1)}, u32[]{:S(2)}, u32[]{:S(2)}) collective-permute-start(bf16[128,256]{1,0:T(8,128)(2,1)} %get-tuple-element.39), channel_id=1, source_target_pairs={{0,10},{1,11},{2,8},{3,9},{4,14},{5,15},{6,12},{7,13},{8,2},{9,3},... | collective-permute-start | bytes 196616 | tf_op jit(solution)/shard_map/ppermute | solution.py:116
  27.5 13.4 %collective-permute-start.7 = (bf16[128,256]{1,0:T(8,128)(2,1)S(1)}, bf16[128,256]{1,0:T(8,128)(2,1)S(1)}, u32[]{:S(2)}, u32[]{:S(2)}) collective-permute-start(bf16[128,256]{1,0:T(8,128)(2,1)S(1)} %get-tuple-element.40), channel_id=1, source_target_pairs={{0,12},{1,13},{2,14},{3,15},{4,8},{5,9},{6,10},{7,11},{8,4},{9,5},... | collective-permute-start | bytes 196616 | tf_op jit(solution)/shard_map/ppermute | solution.py:116
  29.3 11.7 %collective-permute-start.8 = (bf16[128,256]{1,0:T(8,128)(2,1)S(1)}, bf16[128,256]{1,0:T(8,128)(2,1)S(1)}, u32[]{:S(2)}, u32[]{:S(2)}) collective-permute-start(bf16[128,256]{1,0:T(8,128)(2,1)S(1)} %get-tuple-element.41), channel_id=1, source_target_pairs={{0,14},{1,15},{2,12},{3,13},{4,10},{5,11},{6,8},{7,9},{8,6},{9,7},... | collective-permute-start | bytes 196616 | tf_op jit(solution)/shard_map/ppermute | solution.py:116
  33.9 0.7 %copy-start.3 = (bf16[2,256,256]{2,1,0:T(8,128)(2,1)}, bf16[2,256,256]{2,1,0:T(8,128)(2,1)S(1)}, u32[]{:S(2)}) copy-start(bf16[2,256,256]{2,1,0:T(8,128)(2,1)S(1)} %get-tuple-element.51) | copy-start | bytes 786436
  34.6 11.3 %copy-start.4 = (f32[1,2]{1,0:T(1,128)S(1)}, f32[1,2]{1,0:T(1,128)}, u32[]{:S(2)}) copy-start(f32[1,2]{1,0:T(1,128)} %shift_ref.1) | copy-start | bytes 28
  34.6 9.2 %collective-permute-start.14 = (bf16[256,128]{1,0:T(8,128)(2,1)}, bf16[256,128]{1,0:T(8,128)(2,1)S(1)}, u32[]{:S(2)}, u32[]{:S(2)}) collective-permute-start(bf16[256,128]{1,0:T(8,128)(2,1)} %get-tuple-element.49), channel_id=1, source_target_pairs={{0,1},{1,2},{2,3},{3,4},{4,5},{5,6},{6,7},{7,8},{8,9},{9,10},{10,1... | collective-permute-start | bytes 196616 | tf_op jit(solution)/shard_map/ppermute | solution.py:382
  36.6 7.7 %collective-permute-start.15 = (bf16[256,128]{1,0:T(8,128)(2,1)}, bf16[256,128]{1,0:T(8,128)(2,1)S(1)}, u32[]{:S(2)}, u32[]{:S(2)}) collective-permute-start(bf16[256,128]{1,0:T(8,128)(2,1)} %get-tuple-element.50), channel_id=1, source_target_pairs={{1,0},{2,1},{3,2},{4,3},{5,4},{6,5},{7,6},{8,7},{9,8},{10,9},{11,1... | collective-permute-start | bytes 196616 | tf_op jit(solution)/shard_map/ppermute | solution.py:383
  40.4 5.4 %copy-start.2 = (bf16[1,544,512]{2,1,0:T(8,128)(2,1)S(1)}, bf16[1,544,512]{2,1,0:T(8,128)(2,1)}, u32[]{:S(2)}) copy-start(bf16[1,544,512]{2,1,0:T(8,128)(2,1)} %range_ref.1) | copy-start | bytes 1671172
  40.4 16.2 %collective-permute-start.16 = (bf16[2,256,256]{2,1,0:T(8,128)(2,1)}, bf16[2,256,256]{2,1,0:T(8,128)(2,1)S(1)}, u32[]{:S(2)}, u32[]{:S(2)}) collective-permute-start(bf16[2,256,256]{2,1,0:T(8,128)(2,1)} %copy-done.3), channel_id=1, source_target_pairs={{0,16},{16,0},{1,17},{17,1},{2,18},{18,2},{3,19},{19,3},{4,20},{20... | collective-permute-start | bytes 786440 | tf_op jit(solution)/shard_map/ppermute | solution.py:389
  42.2 14.3 %copy-start = (bf16[1,2,512,256]{3,2,1,0:T(8,128)(2,1)S(1)}, bf16[1,2,512,256]{3,2,1,0:T(8,128)(2,1)}, u32[]{:S(2)}) copy-start(bf16[1,2,512,256]{3,2,1,0:T(8,128)(2,1)} %matrix_ref.3) | copy-start | bytes 1572868
  42.2 16.4 %collective-permute-start.9 = (bf16[2,256,256]{2,1,0:T(8,128)(2,1)S(1)}, bf16[2,256,256]{2,1,0:T(8,128)(2,1)S(1)}, u32[]{:S(2)}, u32[]{:S(2)}) collective-permute-start(bf16[2,256,256]{2,1,0:T(8,128)(2,1)S(1)} %get-tuple-element.42), channel_id=1, source_target_pairs={{0,16},{16,0},{1,17},{17,1},{2,18},{18,2},{3,19},{19,3},{4,20},{20... | collective-permute-start | bytes 786440 | tf_op jit(solution)/shard_map/ppermute | solution.py:389
  43.8 12.0 %collective-permute-start.17 = (bf16[256,128]{1,0:T(8,128)(2,1)S(1)}, bf16[256,128]{1,0:T(8,128)(2,1)S(1)}, u32[]{:S(2)}, u32[]{:S(2)}) collective-permute-start(bf16[256,128]{1,0:T(8,128)(2,1)S(1)} %collective-permute-done.14.rim_low), channel_id=1, source_target_pairs={{0,16},{16,0},{1,17},{17,1},{2,18},{18,2},{3,19},{19,3},{4,20},{20... | collective-permute-start | bytes 196616 | tf_op jit(solution)/shard_map/ppermute | solution.py:389
  44.3 12.2 %collective-permute-start.18 = (bf16[256,128]{1,0:T(8,128)(2,1)S(1)}, bf16[256,128]{1,0:T(8,128)(2,1)S(1)}, u32[]{:S(2)}, u32[]{:S(2)}) collective-permute-start(bf16[256,128]{1,0:T(8,128)(2,1)S(1)} %collective-permute-done.15.rim_high), channel_id=1, source_target_pairs={{0,16},{16,0},{1,17},{17,1},{2,18},{18,2},{3,19},{19,3},{4,20},{20... | collective-permute-start | bytes 196616 | tf_op jit(solution)/shard_map/ppermute | solution.py:389
